TPU v7x, 512 devices: a whole 4x4x16 slice. The times are simulated.
512 devices in a mesh: dp: 2 (over z_hi), row: 32 (over z_lo, y), col: 8 (over x, core).
Axes of the slice: x: 4, y: 4, z: 16 (z_hi: 2, z_lo: 8; z = z_hi * 8 + z_lo), core: 2. Of those that a mesh axis runs over, the one named last changes fastest.
Arguments:
- finals: bfloat16 [2048, 4096], P('dp', 'col'), may hold values from -16 to 16
- head_weight: bfloat16 [16384, 4096], P('row', 'col'), may hold values from -0.234375 to 0.234375
- hidden: bfloat16 [2048, 10240], P('dp', 'row'), may hold values from -6 to 6
- targets: int32 [2048], P('dp'), may hold values from 0 to 16383
- head_rows_old: float32 [16384], P('row'), may hold values from 1e-06 to 0.09
- head_cols_old: float32 [4096], P('col'), may hold values from 0.00025 to 0.0075
- down_rows_old: float32 [10240], P('row'), may hold values from 0.05 to 3
- down_cols_old: float32 [4096], P('col'), may hold values from 0.05 to 1.5
Outputs:
- head_update: float32 [16384, 4096], P('row', 'col')
- head_rows: float32 [16384], P('row')
- head_cols: float32 [4096], P('col')
- down_update: float32 [10240, 4096], P('row', 'col')
- down_rows: float32 [10240], P('row')
- down_cols: float32 [4096], P('col')
All inputs are finite; a program needn't handle non-finite values.
Results may differ from a plain program's by a relative error of at most 0.003.
Values may be sent and summed in bfloat16 or wider, within the bound.
A program may use at most 64 MiB of HBM per device.

v0:
```python
import jax
import jax.numpy as jnp
from jax import lax
from jax.sharding import PartitionSpec as P

EPS_SQUARE = 1e-30
DECAY_RATE = 1.0 - 10.0 ** (-0.8)
CLIP_LEVEL = 1.0


def contract_rows(left_side, right_side):
    return lax.dot_general(
        left_side, right_side, (((0,), (0,)), ((), ())), preferred_element_type=jnp.float32
    )


def contract_cols(left_side, right_side):
    return lax.dot_general(
        left_side, right_side, (((1,), (1,)), ((), ())), preferred_element_type=jnp.float32
    )


def softmax_grad(logits, own_targets, vocab_start):
    local_max = jnp.max(logits, axis=1)
    row_max = lax.pmax(local_max, "row")
    shifted = jnp.exp(logits - row_max[:, None])
    row_sum = lax.psum(jnp.sum(shifted, axis=1), "row")
    vocab_ids = vocab_start + jnp.arange(logits.shape[1], dtype=jnp.int32)
    onehot = (own_targets[:, None] == vocab_ids[None, :]).astype(jnp.float32)
    return (shifted / row_sum[:, None] - onehot).astype(jnp.bfloat16)


def new_factors(gradient, row_total, col_total, rows_old, cols_old):
    col_number = gradient.shape[1] * lax.axis_size("col")
    row_number = gradient.shape[0] * lax.axis_size("row")
    rows_new = DECAY_RATE * rows_old + (1.0 - DECAY_RATE) * (row_total / col_number)
    cols_new = DECAY_RATE * cols_old + (1.0 - DECAY_RATE) * (col_total / row_number)
    return (rows_new, cols_new)


def scaled_update(gradient, rows_new, cols_new):
    raw_update = gradient / jnp.sqrt(rows_new[:, None] * cols_new[None, :])
    return (raw_update, jnp.sum(raw_update * raw_update))


def clipped_update(raw_update, square_total):
    entries = (
        raw_update.shape[0] * lax.axis_size("row") * raw_update.shape[1] * lax.axis_size("col")
    )
    rms_ratio = jnp.sqrt(square_total / entries) / CLIP_LEVEL
    return raw_update / jnp.maximum(1.0, rms_ratio)


def single_step(gradient, rows_old, cols_old):
    squares = gradient * gradient + EPS_SQUARE
    row_total = lax.psum(jnp.sum(squares, axis=1), "col")
    col_total = lax.psum(jnp.sum(squares, axis=0), "row")
    rows_new, cols_new = new_factors(gradient, row_total, col_total, rows_old, cols_old)
    raw_update, local_square = scaled_update(gradient, rows_new, cols_new)
    square_total = lax.psum(local_square, ("row", "col"))
    return (clipped_update(raw_update, square_total), rows_new, cols_new)


def local(
    finals, head_weight, hidden, targets, head_rows_old, head_cols_old, down_rows_old, down_cols_old
):
    vocab_rows = head_weight.shape[0]
    vocab_start = lax.axis_index("row") * vocab_rows
    logits = lax.psum(contract_cols(finals, head_weight), "col")
    dlogits = softmax_grad(logits, targets, vocab_start)
    head_grad = lax.psum(contract_rows(dlogits, finals), "dp")
    row_block = dlogits
    dfinals = lax.psum_scatter(
        jnp.dot(row_block, head_weight, preferred_element_type=jnp.float32),
        "row",
        scatter_dimension=0,
        tiled=True,
    ).astype(jnp.bfloat16)
    row_block = hidden
    down_part = contract_rows(row_block, lax.all_gather(dfinals, "row", axis=0, tiled=True))
    down_grad = lax.psum(down_part, "dp")
    head_update, head_rows, head_cols = single_step(head_grad, head_rows_old, head_cols_old)
    down_update, down_rows, down_cols = single_step(down_grad, down_rows_old, down_cols_old)
    return (head_update, head_rows, head_cols, down_update, down_rows, down_cols)


def solution(mesh):
    return jax.shard_map(
        local,
        mesh=mesh,
        in_specs=(
            P("dp", "col"),
            P("row", "col"),
            P("dp", "row"),
            P("dp"),
            P("row"),
            P("col"),
            P("row"),
            P("col"),
        ),
        out_specs=(P("row", "col"), P("row"), P("col"), P("row", "col"), P("row"), P("col")),
        check_vma=False,
    )
```

profile of v0, /device:TPU:1, one launch (start us, length us, event | category | flops | bytes accessed | tf_op | source)
XLA Modules:
  0.0 2103.9 jit_solution(14292002134168224903)
XLA Ops:
  7.2 0.0 all-reduce.7.cloned.1.call-start
  7.2 1.2 copy-done
  8.4 3.1 fusion.7
  11.5 0.0 reduce-scatter.2.cloned.1.call-start
  11.6 84.7 %all-reduce.7.cloned.1.call-done = f32[1024,512]{1,0:T(8,128)} async-done(((f32[1024,512]{1,0:T(8,128)}), f32[1024,512]{1,0:T(8,128)}) %all-reduce.7.cloned.1.call-update) | async-done | bytes 2097168 | tf_op jit(solution)/shard_map/psum | solution.py:69
  96.3 2.0 reduce_max.9
  98.3 109.3 %pmax.7 = f32[1024]{0:T(1024)S(1)} all-reduce(f32[1024]{0:T(1024)S(1)} %reduce_max.9), channel_id=1, replica_groups=mesh['dp'=2,'row'=32,'col'=8] {'row'}, use_global_device_ids=true, to_apply=%region_2.0 | all-reduce | flops 1024 | bytes 8192 | tf_op jit(solution)/shard_map/pmax | solution.py:25
  207.5 0.7 fusion
  208.2 98.9 %psum.71 = f32[1024]{0:T(1024)S(1)} all-reduce(f32[1024]{0:T(1024)S(1)} %fusion), channel_id=1, replica_groups=mesh['dp'=2,'row'=32,'col'=8] {'row'}, use_global_device_ids=true, to_apply=%region_4.0 | all-reduce | flops 1024 | bytes 8192 | tf_op jit(solution)/shard_map/psum | solution.py:27
  307.2 0.9 subtract_convert_fusion
  308.0 1.0 copy-done.4
  309.0 2.1 fusion.9
  311.1 0.0 reduce-scatter.2.cloned.1.call-update
  311.1 0.0 all-gather.2.cloned.1.call-start
  311.1 238.2 %reduce-scatter.2.cloned.1.call-done = f32[32,512]{1,0:T(8,128)} async-done(((f32[1024,512]{1,0:T(8,128)}), f32[32,512]{1,0:T(8,128)}) %reduce-scatter.2.cloned.1.call-update) | async-done | bytes 65552 | tf_op jit(solution)/shard_map/reduce_scatter | solution.py:73
  549.3 1.5 convert_element_type.11
  550.8 0.0 all-gather.2.cloned.1.call-update
  550.8 0.0 all-reduce.9.cloned.1.call-start
  550.9 1.7 fusion.8
  552.6 216.9 %all-gather.2.cloned.1.call-done = bf16[1024,512]{1,0:T(8,128)(2,1)} async-done(((bf16[32,512]{1,0:T(8,128)(2,1)}), bf16[1024,512]{1,0:T(8,128)(2,1)}) %all-gather.2.cloned.1.call-update) | async-done | bytes 1048592 | tf_op jit(solution)/shard_map/all_gather | solution.py:80
  769.5 2.6 convolution_bitcast_fusion
  772.1 0.0 all-reduce.9.cloned.1.call-update
  772.1 210.7 %all-reduce.9.cloned.1.call-done = (f32[512,512]{1,0:T(8,128)}, f32[320,512]{1,0:T(8,128)}) async-done(((f32[512,512]{1,0:T(8,128)}, f32[320,512]{1,0:T(8,128)}), (f32[512,512]{1,0:T(8,128)}, f32[320,512]{1,0:T(8,128)})) %all-reduce.9.cloned.1.call-update) | async-done | bytes 1703952 | tf_op jit(solution)/shard_map/psum | solution.py:71
  982.8 1.6 fusion.2
  984.4 1.3 fusion.5
  985.7 106.1 %all-reduce.1 = (f32[512]{0:T(512)S(1)}, f32[512]{0:T(512)S(1)}) all-reduce(f32[512]{0:T(512)S(1)} %get-tuple-element.7, f32[512]{0:T(512)S(1)} %get-tuple-element.9), channel_id=1, replica_groups=mesh['dp'=2,'row'=32,'col'=8] {'row'}, use_global_device_ids=true, to_apply=%region_9.0 | all-reduce | flops 1024 | bytes 8192 | tf_op jit(solution)/shard_map/psum | solution.py:57
  1091.7 26.7 %all-reduce.2 = (f32[512]{0:T(512)S(1)}, f32[320]{0:T(512)S(1)}) all-reduce(f32[512]{0:T(512)S(1)} %get-tuple-element.6, f32[320]{0:T(512)S(1)} %get-tuple-element.8), channel_id=1, replica_groups=mesh['dp'=2,'row'=32,'col'=8] {'col'}, use_global_device_ids=true, to_apply=%region_7.0 | all-reduce | flops 832 | bytes 6656 | tf_op jit(solution)/shard_map/psum | solution.py:56
  1118.5 1.0 multiply_reduce_fusion
  1119.6 0.9 multiply_reduce_fusion.1
  1120.5 973.2 %all-reduce = (f32[]{:T(128)}, f32[]{:T(128)}) all-reduce(f32[]{:T(128)} %multiply_reduce_fusion, f32[]{:T(128)} %multiply_reduce_fusion.1), channel_id=1, replica_groups=mesh['dp'=2,'row'=32,'col'=8] {'row','col'}, use_global_device_ids=true, to_apply=%region_11.0 | all-reduce | flops 2 | bytes 16 | tf_op jit(solution)/shard_map/psum | solution.py:60
  2094.4 1.0 fusion.6
  2096.1 1.2 fusion.3
  (37 shorter events, 0.1 us)
Async XLA Ops:
  7.2 1.2 copy-start
  7.2 89.1 %all-reduce.7.cloned.1.call-start = ((), (), s32[]{:S(2)}) async-start(), calls=%async_computation.1 | async-start | bytes 4194304 | tf_op jit(solution)/shard_map/psum | solution.py:69
  11.5 537.8 %reduce-scatter.2.cloned.1.call-start = ((), (), s32[]{:S(2)}) async-start(), calls=%async_computation.2 | async-start | bytes 2162688 | tf_op jit(solution)/shard_map/reduce_scatter | solution.py:73
  11.6 295.6 %copy-start.12 = (s32[1024]{0:T(1024)S(1)}, s32[1024]{0:T(1024)}, u32[]{:S(2)}) copy-start(s32[1024]{0:T(1024)} %param.11) | copy-start | bytes 12292
  96.3 111.2 %copy-start.1 = (f32[1024,512]{1,0:T(8,128)S(1)}, f32[1024,512]{1,0:T(8,128)}, u32[]{:S(2)}) copy-start(f32[1024,512]{1,0:T(8,128)} %all-reduce.7.cloned.1.call-done) | copy-start | bytes 6291460
  307.1 1.8 copy-start.6
  308.0 1.0 copy-start.4
  311.0 239.8 %copy-start.5 = (bf16[1024,512]{1,0:T(8,128)(2,1)S(1)}, bf16[1024,512]{1,0:T(8,128)(2,1)}, u32[]{:S(2)}) copy-start(bf16[1024,512]{1,0:T(8,128)(2,1)} %copy-done.4) | copy-start | bytes 3145732
  311.1 458.4 %all-gather.2.cloned.1.call-start = ((), (), s32[]{:S(2)}) async-start(), calls=%async_computation.3 | async-start | bytes 1081344 | tf_op jit(solution)/shard_map/all_gather | solution.py:80
  550.8 218.7 %copy-start.7 = (bf16[1024,320]{0,1:T(8,128)(2,1)S(1)}, bf16[1024,320]{0,1:T(8,128)(2,1)}, u32[]{:S(2)}) copy-start(bf16[1024,320]{0,1:T(8,128)(2,1)} %param.10) | copy-start | bytes 1966084
  550.8 432.0 %all-reduce.9.cloned.1.call-start = ((), (), s32[]{:S(2)}) async-start(), calls=%async_computation.4 | async-start | bytes 3407872 | tf_op jit(solution)/shard_map/psum | solution.py:71
  772.1 346.3 %copy-start.13 = (f32[320]{0:T(512)S(1)}, f32[320]{0:T(512)}, u32[]{:S(2)}) copy-start(f32[320]{0:T(512)} %param.14) | copy-start | bytes 3844
  772.1 346.4 %copy-start.14 = (f32[512]{0:T(512)S(1)}, f32[512]{0:T(512)}, u32[]{:S(2)}) copy-start(f32[512]{0:T(512)} %param.12) | copy-start | bytes 6148
  772.1 346.4 %copy-start.15 = (f32[512]{0:T(512)S(1)}, f32[512]{0:T(512)}, u32[]{:S(2)}) copy-start(f32[512]{0:T(512)} %param.15) | copy-start | bytes 6148
  772.1 346.4 %copy-start.16 = (f32[512]{0:T(512)S(1)}, f32[512]{0:T(512)}, u32[]{:S(2)}) copy-start(f32[512]{0:T(512)} %param.13) | copy-start | bytes 6148
  982.8 135.7 %copy-start.2 = (f32[512,512]{1,0:T(8,128)S(1)}, f32[512,512]{1,0:T(8,128)}, u32[]{:S(2)}) copy-start(f32[512,512]{1,0:T(8,128)} %get-tuple-element.16) | copy-start | bytes 3145732
  982.8 136.8 %copy-start.3 = (f32[320,512]{1,0:T(8,128)S(1)}, f32[320,512]{1,0:T(8,128)}, u32[]{:S(2)}) copy-start(f32[320,512]{1,0:T(8,128)} %get-tuple-element.17) | copy-start | bytes 1966084
  1118.4 978.9 %copy-start.8 = (f32[320]{0:T(512)}, f32[320]{0:T(512)S(1)}, u32[]{:S(2)}) copy-start(f32[320]{0:T(512)S(1)} %multiply_add_fusion.3) | copy-start | bytes 3844
  1118.4 978.9 %copy-start.9 = (f32[512]{0:T(512)}, f32[512]{0:T(512)S(1)}, u32[]{:S(2)}) copy-start(f32[512]{0:T(512)S(1)} %multiply_add_fusion.5) | copy-start | bytes 6148
  1118.5 978.8 %copy-start.10 = (f32[512]{0:T(512)}, f32[512]{0:T(512)S(1)}, u32[]{:S(2)}) copy-start(f32[512]{0:T(512)S(1)} %get-tuple-element.18) | copy-start | bytes 6148
  1118.5 978.8 %copy-start.11 = (f32[512]{0:T(512)}, f32[512]{0:T(512)S(1)}, u32[]{:S(2)}) copy-start(f32[512]{0:T(512)S(1)} %get-tuple-element.19) | copy-start | bytes 6148
Sparse Core Ops, SparseCore 0:
  11.6 84.6 all-reduce.6
  311.2 238.0 reduce-scatter.1
  552.2 217.2 all-gather.1
  773.1 209.6 all-reduce.8
where the time goes:
time: 2100 us
  blocking collectives  1310 us (62%)
  waiting for transfers between devices  751 us (36%)
    psum x1, blocking collectives, single_step(): square_total = lax.psum(local_square, ('row', 'col'))  973 us
    reduce_scatter x1, waiting for transfers between devices, local(): lax.psum_scatter(jnp.dot(row_block, head_weight, preferred_element_type=j...  238 us
    all_gather x1, waiting for transfers between devices, local(): lax.all_gather(dfinals, 'row', axis=0, tiled=True)  217 us
    psum x1, waiting for transfers between devices, local(): head_grad = lax.psum(contract_rows(dlogits, finals), 'dp')  211 us
    pmax x1, blocking collectives, softmax_grad(): row_max = lax.pmax(local_max, 'row')  109 us
    psum x1, blocking collectives, single_step(): col_total = lax.psum(jnp.sum(squares, axis=0), 'row')  106 us
    psum x1, blocking collectives, softmax_grad(): row_sum = lax.psum(jnp.sum(shifted, axis=1), 'row')  98.9 us
    psum x1, waiting for transfers between devices, local(): logits = lax.psum(contract_cols(finals, head_weight), 'col')  84.7 us
  transfers between devices with their start and end apart: 4, of which 4 were waited for; matrix products, arithmetic and copies ran while one was open for 0% of the time, Pallas kernels for 0%

commit v1 on v0

v1 whole, which is shorter than its diff:
```python
import jax
import jax.numpy as jnp
from jax import lax
from jax.experimental import pallas as pl
from jax.experimental.pallas import tpu as pltpu
from jax.sharding import PartitionSpec as P

EPS_SQUARE = 1e-30
DECAY_RATE = 1.0 - 10.0 ** (-0.8)
CLIP_LEVEL = 1.0
F32, BF16, I16 = jnp.float32, jnp.bfloat16, jnp.int16
MESH = pl.DeviceIdType.MESH

NZ, NY, NX = 8, 4, 4
T = 1024
V = 512
D = 512
FF = 320
C = 128
FULL_V, FULL_D, FULL_FF = 16384, 4096, 10240
QD = D // NY
BD = QD // NZ
LIMIT = 32766.0


def tokens_dot(left, right):
    return lax.dot_general(left, right, (((1,), (1,)), ((), ())), preferred_element_type=F32)


def plain_dot(left, right):
    return jnp.dot(left, right, preferred_element_type=F32)


def unit_of(values):
    peak = jnp.max(jnp.abs(values), axis=0, keepdims=True)
    return jnp.maximum(peak, 1e-30) * (1.0 / LIMIT)


def coded(values, unit):
    return jnp.round(values * (1.0 / unit)).astype(jnp.int32).astype(I16)


def decoded(codes, unit):
    return codes.astype(jnp.int32).astype(F32) * unit


def lanes_to_tile(ref, row, vector):
    for part in range(vector.shape[1] // 128):
        ref[pl.ds(row + part, 1), :] = vector[:, 128 * part : 128 * part + 128]


def tile_to_lanes(tile, row, parts):
    return jnp.concatenate([tile[row + p : row + p + 1, :] for p in range(parts)], axis=1)


def column_to_lanes(column):
    return jnp.broadcast_to(column, (column.shape[0], 128)).T[0:1, :]


def lanes_to_column(vector):
    return jnp.broadcast_to(vector, (128, vector.shape[1])).T[:, 0:1]


def body(
    fin_in, w_in, hid_in, tgt, hro, hco, dro, dco,
    hup, hrows, hcols, dup, drows, dcols,
    fin, w, wt, hid, hidt, dl,
    part, core_out, core_in, x_out, x_in, xu_out, xu_in,
    stat, dft, y_out, y_in, yu_out, yu_in, z_out, z_in, zu_out, zu_in,
    dfb, hg, dg, rtile, ctile, ztile, stile,
    local_sem, send_sem, recv_sem,
):
    d, row, col = lax.axis_index("dp"), lax.axis_index("row"), lax.axis_index("col")
    z, y, x, k = row // NY, row % NY, col // 2, col % 2
    zz = d * NZ + z
    od = 1 - d

    def at(dd, z_, y_, c_):
        return (dd, z_ * NY + y_, c_)

    def ring(o):
        q = (zz + o) % (2 * NZ)
        return at(q // NZ, q % NZ, y, col)

    def x_peer(o):
        return (d, row, ((x + o) % NX) * 2 + k)

    def y_peer(o):
        return at(d, z, (y + o) % NY, col)

    def z_peer(o):
        return at(d, (z + o) % NZ, y, col)

    core = (d, row, 2 * x + 1 - k)
    dp_peer = (od, row, col)
    mirror = at(od, NZ - 1 - z, y, col)

    pending = []
    count = [0]

    def remote(src, dst, device, slot=None):
        if slot is None:
            slot = count[0]
            count[0] += 1
        copy = pltpu.make_async_remote_copy(
            src_ref=src, dst_ref=dst, send_sem=send_sem.at[slot], recv_sem=recv_sem.at[slot],
            device_id=device, device_id_type=MESH,
        )
        copy.start()
        pending.append(copy)
        return copy

    loads = [
        pltpu.make_async_copy(fin_in, fin.at[pl.ds(d * T, T), :], local_sem.at[0]),
        pltpu.make_async_copy(w_in, w, local_sem.at[1]),
        pltpu.make_async_copy(hid_in, hid.at[pl.ds(d * T, T), :], local_sem.at[2]),
    ]
    for load in loads:
        load.start()

    barrier = pltpu.get_barrier_semaphore()

    def greet(device):
        pl.semaphore_signal(barrier, inc=1, device_id=device, device_id_type=MESH)

    @pl.loop(1, 32)
    def _(o):
        greet((d, (row + o) % 32, col))

    @pl.loop(1, 8)
    def _(o):
        greet((d, row, (col + o) % 8))

    others = [dp_peer, mirror] + [ring(o) for o in (1, -1, 2, -2, 4, -4)]
    for device in others:
        greet(device)
    pl.semaphore_wait(barrier, 31 + 7 + len(others))
    for load in loads:
        load.wait()

    fq = pl.multiple_of(d * T + (y * NZ + z) * 32, 32)
    fin_cross = remote(fin.at[pl.ds(fq, 32), :], fin.at[pl.ds(fq, 32), :], mirror)
    hq = pl.multiple_of(d * T + col * C, C)
    hid_cross = remote(hid.at[pl.ds(hq, C), :], hid.at[pl.ds(hq, C), :], dp_peer)

    def logits_part(c):
        start = pl.multiple_of(d * T + c * C, C)
        return tokens_dot(w[...], fin[pl.ds(start, C), :])

    core_copies = {}
    for o in (1, 2, 3, 0):
        xo = (x + o) % NX
        core_out[o] = logits_part(2 * xo + 1 - k)
        core_copies[o] = remote(core_out.at[o], core_in.at[o], core)
    for o in (1, 2, 3, 0):
        xo = (x + o) % NX
        part[o] = logits_part(2 * xo + k)
    x_copies = []
    for o in (1, 2, 3):
        core_copies[o].wait_recv()
        total = part[o] + core_in[o]
        unit = unit_of(total)
        x_out[o - 1] = coded(total, unit)
        xu_out[o - 1] = unit
        x_copies.append(remote(x_out.at[o - 1], x_in.at[o - 1], x_peer(o)))
        x_copies.append(remote(xu_out.at[o - 1], xu_in.at[o - 1], x_peer(o)))
    core_copies[0].wait_recv()
    part[0] = part[0] + core_in[0]
    wt[...] = w[...].T

    fin_cross.wait_recv()
    gq = pl.multiple_of(od * T + (y * NZ + NZ - 1 - z) * 32, 32)
    fin_z = [
        remote(fin.at[pl.ds(gq, 32), :], fin.at[pl.ds(gq, 32), :], z_peer(o)) for o in range(1, NZ)
    ]

    for copy in x_copies:
        copy.wait_recv()
    logits = part[0]
    for o in (1, 2, 3):
        logits = logits + decoded(x_in[o - 1], xu_in[o - 1])
    part[0] = logits

    top = jnp.max(logits, axis=0, keepdims=True)
    total = jnp.sum(jnp.exp(logits - top), axis=0, keepdims=True)
    stat[row, 0:1, :] = top
    stat[row, 1:2, :] = total
    base = count[0]
    count[0] += 31

    def stat_copy(o):
        return pltpu.make_async_remote_copy(
            src_ref=stat.at[row], dst_ref=stat.at[row],
            send_sem=send_sem.at[base + o - 1], recv_sem=recv_sem.at[base + o - 1],
            device_id=(d, (row + o) % 32, col), device_id_type=MESH,
        )

    @pl.loop(1, 32)
    def _(o):
        stat_copy(o).start()

    @pl.loop(1, 32)
    def _(o):
        stat_copy(o).wait_recv()

    stats = stat[...]
    tops, totals = stats[:, 0:1, :], stats[:, 1:2, :]
    row_max = jnp.max(tops, axis=0)
    row_sum = jnp.sum(totals * jnp.exp(tops - row_max[None]), axis=0)
    ids = row * V + lax.broadcasted_iota(jnp.int32, (V, C), 0)
    onehot = (tgt[pl.ds(col, 1), :] == ids).astype(F32)
    dlogits = jnp.exp(part[0] - row_max) / row_sum - onehot
    me = d * 8 + col
    dl[me] = dlogits.astype(BF16)

    def spread_x(half, c):
        slot = half * 8 + c
        first = [remote(dl.at[slot], dl.at[slot], x_peer(o)) for o in (1, 2, 3)]
        return first + [remote(dl.at[slot], dl.at[slot], core)]

    def spread_core(half, copies):
        passed = [copies[3]]
        for o in (1, 2, 3):
            copies[o - 1].wait_recv()
            slot = half * 8 + ((x - o) % NX) * 2 + k
            passed.append(remote(dl.at[slot], dl.at[slot], core))
        return passed

    own_x = spread_x(d, col)
    dl_cross = remote(dl.at[me], dl.at[me], dp_peer)
    own_core = spread_core(d, own_x)
    for copy in own_core:
        copy.wait_recv()

    @pl.loop(0, 8)
    def _(c):
        piece = plain_dot(wt[...], dl[d * 8 + c])
        unit = unit_of(piece)
        lanes = pl.ds(pl.multiple_of(c * C, C), C)
        dft[:, lanes] = piece
        y_out[:, lanes] = coded(piece, unit)
        yu_out[:, lanes] = unit

    y_copies = []
    for o in (1, 2, 3):
        quarter = pl.ds(pl.multiple_of(((y + o) % NY) * QD, QD), QD)
        y_copies.append(remote(y_out.at[quarter, :], y_in.at[o - 1], y_peer(o)))
        y_copies.append(remote(yu_out, yu_in.at[o - 1], y_peer(o)))

    hid_cross.wait_recv()
    ho = pl.multiple_of(od * T + col * C, C)
    hid_cols = [
        remote(hid.at[pl.ds(ho, C), :], hid.at[pl.ds(ho, C), :], (d, row, (col + o) % 8))
        for o in range(1, 8)
    ]

    for copy in y_copies:
        copy.wait_recv()
    quarter = dft[pl.ds(pl.multiple_of(y * QD, QD), QD), :]
    for o in (1, 2, 3):
        quarter = quarter + decoded(y_in[o - 1], yu_in[o - 1])
    dft[0:QD, :] = quarter
    unit = unit_of(quarter)
    zu_out[...] = unit
    z_out[...] = coded(quarter, unit)
    z_copies = []
    for o in range(1, NZ):
        block = pl.ds(pl.multiple_of(((z + o) % NZ) * BD, BD), BD)
        z_copies.append(remote(z_out.at[block, :], z_in.at[o - 1], z_peer(o)))
        z_copies.append(remote(zu_out, zu_in.at[o - 1], z_peer(o)))

    for copy in fin_z:
        copy.wait_recv()
    gy = pl.multiple_of(od * T + y * 256, 256)
    fin_y = [
        remote(fin.at[pl.ds(gy, 256), :], fin.at[pl.ds(gy, 256), :], y_peer(o)) for o in (1, 2, 3)
    ]
    dl_cross.wait_recv()
    other_x = spread_x(od, col)

    for copy in z_copies:
        copy.wait_recv()
    block = dft[pl.ds(pl.multiple_of(z * BD, BD), BD), :]
    for o in range(1, NZ):
        block = block + decoded(z_in[o - 1], zu_in[o - 1])
    dfb[y, zz] = block.astype(BF16)

    far = [remote(dfb.at[y, zz], dfb.at[y, zz], ring(o)) for o in (4, 8, -4)]
    other_core = spread_core(od, other_x)
    for copy in hid_cols:
        copy.wait_recv()
    for half in range(2):
        hidt[half] = hid[half * T : half * T + T, :].T
    for copy in far:
        copy.wait_recv()
    near = []
    for o in (1, -1, 2):
        for q in range(4):
            b = (zz + 4 * q) % (2 * NZ)
            near.append(remote(dfb.at[y, b], dfb.at[y, b], ring(o)))
    for copy in near:
        copy.wait_recv()
    along_y = [remote(dfb.at[y], dfb.at[y], y_peer(o)) for o in (1, 2, 3)]

    for copy in fin_y + other_core:
        copy.wait_recv()
    hg[...] = jnp.zeros_like(hg)

    @pl.loop(0, 16)
    def _(c):
        start = pl.multiple_of(c * C, C)
        hg[...] += plain_dot(dl[c], fin[pl.ds(start, C), :])

    for copy in along_y:
        copy.wait_recv()
    dg[...] = tokens_dot(hidt[0], dfb[:, 0:NZ].reshape(D, T)) + tokens_dot(
        hidt[1], dfb[:, NZ : 2 * NZ].reshape(D, T)
    )

    rtile[col] = jnp.zeros((8, 128), F32)
    hsq = hg[...] * hg[...]
    dsq = dg[...] * dg[...]
    mine = rtile.at[col]
    lanes_to_tile(mine, 0, column_to_lanes(jnp.sum(hsq, axis=1, keepdims=True)))
    down_lanes = column_to_lanes(jnp.sum(dsq, axis=1, keepdims=True))
    mine[4:5, :] = down_lanes[:, 0:128]
    mine[5:6, :] = down_lanes[:, 128:256]
    mine[6:7, 0:64] = down_lanes[:, 256:320]
    copies = [remote(rtile.at[col], rtile.at[col], (d, row, (col + o) % 8)) for o in range(1, 8)]
    for copy in copies:
        copy.wait_recv()
    rsum = jnp.sum(rtile[...], axis=0)
    hr = DECAY_RATE * hro[...] + (1.0 - DECAY_RATE) * (
        tile_to_lanes(rsum, 0, 4) * (1.0 / FULL_D) + EPS_SQUARE
    )
    dr = DECAY_RATE * dro[...] + (1.0 - DECAY_RATE) * (
        tile_to_lanes(rsum, 4, 3)[:, 0:FF] * (1.0 / FULL_D) + EPS_SQUARE
    )
    hrows[...] = hr
    drows[...] = dr
    hr_col = lanes_to_column(hr)
    dr_col = lanes_to_column(dr)

    mine = ctile.at[y]
    lanes_to_tile(mine, 0, jnp.sum(hsq, axis=0, keepdims=True))
    lanes_to_tile(mine, 4, jnp.sum(dsq, axis=0, keepdims=True))
    lanes_to_tile(mine, 8, jnp.sum(hsq / hr_col, axis=0, keepdims=True))
    lanes_to_tile(mine, 12, jnp.sum(dsq / dr_col, axis=0, keepdims=True))
    copies = [remote(ctile.at[y], ctile.at[y], y_peer(o)) for o in (1, 2, 3)]
    for copy in copies:
        copy.wait_recv()
    ztile[z] = jnp.sum(ctile[...], axis=0)
    copies = [remote(ztile.at[z], ztile.at[z], z_peer(o)) for o in range(1, NZ)]
    for copy in copies:
        copy.wait_recv()
    csum = jnp.sum(ztile[...], axis=0)
    hc = DECAY_RATE * hco[...] + (1.0 - DECAY_RATE) * (
        tile_to_lanes(csum, 0, 4) * (1.0 / FULL_V) + EPS_SQUARE
    )
    dc = DECAY_RATE * dco[...] + (1.0 - DECAY_RATE) * (
        tile_to_lanes(csum, 4, 4) * (1.0 / FULL_FF) + EPS_SQUARE
    )
    hcols[...] = hc
    dcols[...] = dc
    hs = jnp.sum(tile_to_lanes(csum, 8, 4) / hc, axis=1, keepdims=True)
    ds = jnp.sum(tile_to_lanes(csum, 12, 4) / dc, axis=1, keepdims=True)
    stile[col, 0:1, :] = jnp.broadcast_to(hs, (1, 128))
    stile[col, 1:2, :] = jnp.broadcast_to(ds, (1, 128))
    copies = [remote(stile.at[col], stile.at[col], (d, row, (col + o) % 8)) for o in range(1, 8)]
    hup[...] = hg[...] * lax.rsqrt(hr_col) * lax.rsqrt(hc)
    dup[...] = dg[...] * lax.rsqrt(dr_col) * lax.rsqrt(dc)
    for copy in copies:
        copy.wait_recv()
    squares = jnp.sum(stile[...], axis=0)

    def clip(square_total, entries):
        return 1.0 / jnp.maximum(1.0, jnp.sqrt(square_total * (1.0 / entries)) / CLIP_LEVEL)

    hup[...] = hup[...] * clip(squares[0:1, 0:1], FULL_V * FULL_D)
    dup[...] = dup[...] * clip(squares[1:2, 0:1], FULL_FF * FULL_D)

    for copy in pending:
        copy.wait_send()

    @pl.loop(1, 32)
    def _(o):
        stat_copy(o).wait_send()


N_SEM = 160


def local(fin, w, hid, tgt, hro, hco, dro, dco):
    sds = jax.ShapeDtypeStruct
    vm = pltpu.VMEM
    hbm = pl.BlockSpec(memory_space=pl.ANY)
    vmem = pl.BlockSpec(memory_space=pltpu.VMEM)
    out = pl.pallas_call(
        body,
        out_shape=(
            sds((V, D), F32), sds((1, V), F32), sds((1, D), F32),
            sds((FF, D), F32), sds((1, FF), F32), sds((1, D), F32),
        ),
        in_specs=[hbm] * 3 + [vmem] * 5,
        out_specs=(vmem,) * 6,
        scratch_shapes=[
            vm((2 * T, D), BF16),
            vm((V, D), BF16),
            vm((D, V), BF16),
            vm((2 * T, FF), BF16),
            vm((2, FF, T), BF16),
            vm((16, V, C), BF16),
            vm((4, V, C), F32),
            vm((4, V, C), F32),
            vm((4, V, C), F32),
            vm((3, V, C), I16),
            vm((3, V, C), I16),
            vm((3, 1, C), F32),
            vm((3, 1, C), F32),
            vm((32, 2, C), F32),
            vm((D, T), F32),
            vm((D, T), I16),
            vm((3, QD, T), I16),
            vm((1, T), F32),
            vm((3, 1, T), F32),
            vm((QD, T), I16),
            vm((NZ - 1, BD, T), I16),
            vm((1, T), F32),
            vm((NZ - 1, 1, T), F32),
            vm((NY, 2 * NZ, BD, T), BF16),
            vm((V, D), F32),
            vm((FF, D), F32),
            vm((8, 8, 128), F32),
            vm((NY, 16, 128), F32),
            vm((NZ, 16, 128), F32),
            vm((8, 2, 128), F32),
            pltpu.SemaphoreType.DMA((3,)),
            pltpu.SemaphoreType.DMA((N_SEM,)),
            pltpu.SemaphoreType.DMA((N_SEM,)),
        ],
        compiler_params=pltpu.CompilerParams(
            collective_id=0, has_side_effects=True, vmem_limit_bytes=56 << 20
        ),
    )(
        fin, w, hid, tgt.reshape(8, C), hro.reshape(1, V), hco.reshape(1, D),
        dro.reshape(1, FF), dco.reshape(1, D),
    )
    hup, hrows, hcols, dup, drows, dcols = out
    return (hup, hrows.reshape(V), hcols.reshape(D), dup, drows.reshape(FF), dcols.reshape(D))


def solution(mesh):
    return jax.shard_map(
        local,
        mesh=mesh,
        in_specs=(
            P("dp", "col"),
            P("row", "col"),
            P("dp", "row"),
            P("dp"),
            P("row"),
            P("col"),
            P("row"),
            P("col"),
        ),
        out_specs=(P("row", "col"), P("row"), P("col"), P("row", "col"), P("row"), P("col")),
        check_vma=False,
    )
```

time: 2100 us -> 162 us (0.08)
  blocking collectives: 1310 us -> 0 us
  waiting for transfers between devices: 751 us -> 0 us
  Pallas kernels: 0 us -> 151 us
    psum x4 -> x0, blocking collectives: 1200 us -> none  [the longest x1 973 us: single_step(): square_total = lax.psum(local_square, ('row', 'col'))]
    psum x2 -> x0, waiting for transfers between devices: 295 us -> none  [the longest x1 211 us: local(): head_grad = lax.psum(contract_rows(dlogits, finals), 'dp')]
    reduce_scatter x1 -> x0, waiting for transfers between devices: 238 us -> none  [local(): lax.psum_scatter(jnp.dot(row_block, head_weight, preferred_element_type=j...]
    all_gather x1 -> x0, waiting for transfers between devices: 217 us -> none  [local(): lax.all_gather(dfinals, 'row', axis=0, tiled=True)]
    pallas_call x0 -> x1, Pallas kernels: none -> 151 us  [local(): pl.pallas_call(body, out_shape=(sds((V, D), F32), sds((1, V), F32), sds((...]
    pmax x1 -> x0, blocking collectives: 109 us -> none  [softmax_grad(): row_max = lax.pmax(local_max, 'row')]
  transfers between devices with their start and end apart: 4 -> 0, of which waited for: 4 -> 0; matrix products, arithmetic and copies ran while one was open for 0% -> 0% of each run, Pallas kernels for 0% -> 0%
where the time goes in v1:
time: 162 us
  Pallas kernels  151 us (93%)
  local copies, waits for them, and re-layouts  9.17 us (6%)
    pallas_call x1, Pallas kernels, local(): pl.pallas_call(body, out_shape=(sds((V, D), F32), sds((1, V), F32), sds((...  151 us
    unnamed x18, local copies, waits for them, and re-layouts  8.61 us

profile of v1, /device:TPU:1, one launch (start us, length us, event | category | flops | bytes accessed | tf_op | source)
XLA Modules:
  0.0 161.8 jit_solution(3397181923816378584)
XLA Ops:
  0.6 0.0 copy-start.1
  0.6 0.7 copy-done.1
  1.3 0.6 reshape.42.dro
  1.9 2.2 %copy.14.hid_in = bf16[1024,320]{1,0:T(8,128)(2,1)} copy(bf16[1024,320]{0,1:T(8,128)(2,1)} %param.10) | data formatting | bytes 1310720 | tf_op args[2]
  4.1 151.4 %shard_map.127 = (f32[512,512]{1,0:T(8,128)}, f32[1,512]{1,0:T(1,128)}, f32[1,512]{1,0:T(1,128)}, f32[320,512]{1,0:T(8,128)}, f32[1,320]{1,0:T(1,128)}, /*index=5*/f32[1,512]{1,0:T(1,128)}) custom-call(bf16[1024,512]{1,0:T(8,128)(2,1)} %fin_in.1, bf16[512,512]{1,0:T(8,128)(2,1)} %w_in.1, bf16[1024,320]{1,0:T(8,128)(2,1)} %copy.14.hid_in, s32[8,128]{1,0:T(8,128)} %bitcast.7, ...), custom_call_target="tpu_custom_call" | custom-call | tf_op jit(solution)/shard_map/pallas_call | solution.py:398
  155.5 0.0 copy-start.5
  155.5 0.7 copy-done.5
  156.2 0.6 reduce
  156.8 0.0 copy-start.4
  156.8 0.0 copy-start
  156.8 2.3 %copy.20 = f32[512,512]{1,0:T(8,128)} copy(f32[512,512]{1,0:T(8,128)} %get-tuple-element.24) | data formatting | bytes 2097152
  159.1 0.0 copy-done.4
  159.1 0.0 copy-start.3
  159.1 0.6 copy.21
  159.7 0.1 copy-done.3
  159.8 0.6 copy.22
  160.4 0.0 copy-done
  160.4 0.0 copy-start.2
  160.4 0.8 copy.23
  161.2 0.0 copy-done.2
  161.2 0.6 copy.24
Async XLA Ops:
  0.6 0.7 copy-start.1
  155.5 0.7 copy-start.5
  156.8 2.3 %copy-start.4 = (f32[1,512]{1,0:T(1,128)S(1)}, f32[1,512]{1,0:T(1,128)}, u32[]{:S(2)}) copy-start(f32[1,512]{1,0:T(1,128)} %get-tuple-element.13) | copy-start | bytes 6148
  156.8 3.6 %copy-start = (f32[320,512]{1,0:T(8,128)S(1)}, f32[320,512]{1,0:T(8,128)}, u32[]{:S(2)}) copy-start(f32[320,512]{1,0:T(8,128)} %get-tuple-element.27) | copy-start | bytes 1966084
  159.1 0.7 copy-start.3
  160.4 0.8 copy-start.2

commit v2 on v1

v2 whole, which is shorter than its diff:
```python
import jax
import jax.numpy as jnp
from jax import lax
from jax.experimental import pallas as pl
from jax.experimental.pallas import tpu as pltpu
from jax.sharding import PartitionSpec as P

EPS_SQUARE = 1e-30
DECAY_RATE = 1.0 - 10.0 ** (-0.8)
CLIP_LEVEL = 1.0
F32, BF16, I16 = jnp.float32, jnp.bfloat16, jnp.int16
MESH = pl.DeviceIdType.MESH

NZ, NY, NX = 8, 4, 4
T = 1024
V = 512
D = 512
FF = 320
C = 128
FULL_V, FULL_D, FULL_FF = 16384, 4096, 10240
QD = D // NY
BD = QD // NZ
LIMIT = 32766.0
PARTS = ((0, 1), (3, 2))


def tokens_dot(left, right):
    return lax.dot_general(left, right, (((1,), (1,)), ((), ())), preferred_element_type=F32)


def plain_dot(left, right):
    return jnp.dot(left, right, preferred_element_type=F32)


def unit_of(values):
    peak = jnp.max(jnp.abs(values), axis=0, keepdims=True)
    return jnp.maximum(peak, 1e-30) * (1.0 / LIMIT)


def coded(values, unit):
    return jnp.round(values * (1.0 / unit)).astype(jnp.int32).astype(I16)


def decoded(codes, unit):
    return codes.astype(jnp.int32).astype(F32) * unit


def lanes_to_tile(ref, row, vector):
    for part in range(vector.shape[1] // 128):
        ref[pl.ds(row + part, 1), :] = vector[:, 128 * part : 128 * part + 128]


def tile_to_lanes(tile, row, parts):
    return jnp.concatenate([tile[row + p : row + p + 1, :] for p in range(parts)], axis=1)


def column_to_lanes(column):
    return jnp.broadcast_to(column, (column.shape[0], 128)).T[0:1, :]


def lanes_to_column(vector):
    return jnp.broadcast_to(vector, (128, vector.shape[1])).T[:, 0:1]


def body(
    fin_in, w_in, hid_in, tgt, hro, hco, dro, dco,
    hup, hrows, hcols, dup, drows, dcols, clips,
    fin, w, wt, hid, dl,
    part, core_out, core_in, x_out, x_in, xu_out, xu_in,
    stat, dft, y_out, y_in, yu_out, yu_in, z_out, z_in, zu_out, zu_in,
    dfb, hg, rtile, ctile, ztile, stile,
    local_sem, send_sem, recv_sem,
):
    d, row, col = lax.axis_index("dp"), lax.axis_index("row"), lax.axis_index("col")
    z, y, x, k = row // NY, row % NY, col // 2, col % 2
    zz = d * NZ + z
    od = 1 - d

    def at(dd, z_, y_, c_):
        return (dd, z_ * NY + y_, c_)

    def ring(o):
        q = (zz + o) % (2 * NZ)
        return at(q // NZ, q % NZ, y, col)

    def x_peer(o):
        return (d, row, ((x + o) % NX) * 2 + k)

    def y_peer(o):
        return at(d, z, (y + o) % NY, col)

    def z_peer(o):
        return at(d, (z + o) % NZ, y, col)

    core = (d, row, 2 * x + 1 - k)
    dp_peer = (od, row, col)

    pending = []
    count = [0]

    def remote(src, dst, device, slot=None):
        if slot is None:
            slot = count[0]
            count[0] += 1
        copy = pltpu.make_async_remote_copy(
            src_ref=src, dst_ref=dst, send_sem=send_sem.at[slot], recv_sem=recv_sem.at[slot],
            device_id=device, device_id_type=MESH,
        )
        copy.start()
        pending.append(copy)
        return copy

    loads = [
        pltpu.make_async_copy(fin_in, fin.at[pl.ds(d * T, T), :], local_sem.at[0]),
        pltpu.make_async_copy(w_in, w, local_sem.at[1]),
        pltpu.make_async_copy(hid_in, hid.at[d], local_sem.at[2]),
    ]
    for load in loads:
        load.start()

    barrier = pltpu.get_barrier_semaphore()

    def greet(device):
        pl.semaphore_signal(barrier, inc=1, device_id=device, device_id_type=MESH)

    @pl.loop(1, 32)
    def _(o):
        greet((d, (row + o) % 32, col))

    @pl.loop(1, 8)
    def _(o):
        greet((d, row, (col + o) % 8))

    @pl.loop(0, NZ)
    def _(o):
        greet(at(od, o, y, col))

    for load in loads:
        load.wait()

    def logits_part(c):
        start = pl.multiple_of(d * T + c * C, C)
        return tokens_dot(w[...], fin[pl.ds(start, C), :])

    for o in (1, 2, 3, 0):
        xo = (x + o) % NX
        core_out[o] = logits_part(2 * xo + 1 - k)
        part[o] = logits_part(2 * xo + k)
    wt[...] = w[...].T
    pl.semaphore_wait(barrier, 31 + 7 + NZ)

    core_copies = {}
    for o in (1, 2, 3, 0):
        core_copies[o] = remote(core_out.at[o], core_in.at[o], core)
    fq = pl.multiple_of(d * T + (y * NZ + z) * 32, 32)
    fin_cross = [
        remote(fin.at[pl.ds(fq, 32), :], fin.at[pl.ds(fq, 32), :], at(od, (z + o) % NZ, y, col))
        for o in range(NZ)
    ]
    x_copies = []
    for o in (1, 2, 3):
        core_copies[o].wait_recv()
        total = part[o] + core_in[o]
        unit = unit_of(total)
        x_out[o - 1] = coded(total, unit)
        xu_out[o - 1] = unit
        x_copies.append(remote(x_out.at[o - 1], x_in.at[o - 1], x_peer(o)))
        x_copies.append(remote(xu_out.at[o - 1], xu_in.at[o - 1], x_peer(o)))
    core_copies[0].wait_recv()
    part[0] = part[0] + core_in[0]

    for copy in x_copies:
        copy.wait_recv()
    logits = part[0]
    for o in (1, 2, 3):
        logits = logits + decoded(x_in[o - 1], xu_in[o - 1])
    part[0] = logits

    top = jnp.max(logits, axis=0, keepdims=True)
    total = jnp.sum(jnp.exp(logits - top), axis=0, keepdims=True)
    stat[row, 0:1, :] = top
    stat[row, 1:2, :] = total
    base = count[0]
    count[0] += 31

    def stat_copy(o):
        return pltpu.make_async_remote_copy(
            src_ref=stat.at[row], dst_ref=stat.at[row],
            send_sem=send_sem.at[base + o - 1], recv_sem=recv_sem.at[base + o - 1],
            device_id=(d, (row + o) % 32, col), device_id_type=MESH,
        )

    @pl.loop(1, 32)
    def _(o):
        stat_copy(o).start()

    @pl.loop(1, 32)
    def _(o):
        stat_copy(o).wait_recv()

    stats = stat[...]
    tops, totals = stats[:, 0:1, :], stats[:, 1:2, :]
    row_max = jnp.max(tops, axis=0)
    row_sum = jnp.sum(totals * jnp.exp(tops - row_max[None]), axis=0)
    ids = row * V + lax.broadcasted_iota(jnp.int32, (V, C), 0)
    onehot = (tgt[pl.ds(col, 1), :] == ids).astype(F32)
    dlogits = jnp.exp(part[0] - row_max) / row_sum - onehot
    me = d * 8 + col
    dl[me] = dlogits.astype(BF16)

    def spread_x(half, c):
        slot = half * 8 + c
        first = [remote(dl.at[slot], dl.at[slot], x_peer(o)) for o in (1, 2, 3)]
        return first + [remote(dl.at[slot], dl.at[slot], core)]

    def pass_core(half, copies, o):
        copies[o - 1].wait_recv()
        slot = half * 8 + ((x - o) % NX) * 2 + k
        return remote(dl.at[slot], dl.at[slot], core)

    own_x = spread_x(d, col)
    dl_cross = remote(dl.at[me], dl.at[me], dp_peer)
    hq = pl.ds(pl.multiple_of(col * C, C), C)
    hid_cross = remote(hid.at[d, :, hq], hid.at[d, :, hq], dp_peer)
    own_core = {0: own_x[3]}
    own_core[1] = pass_core(d, own_x, 1)
    for copy in fin_cross:
        copy.wait_recv()
    gy = pl.multiple_of(od * T + y * 256, 256)
    fin_y = [
        remote(fin.at[pl.ds(gy, 256), :], fin.at[pl.ds(gy, 256), :], y_peer(o)) for o in (1, 2, 3)
    ]
    own_core[3] = pass_core(d, own_x, 3)
    own_core[2] = pass_core(d, own_x, 2)

    y_copies = []
    for p, offsets in enumerate(PARTS):
        for j, o in enumerate(offsets):
            own_core[o].wait_recv()
            for core_ in range(2):
                piece = plain_dot(wt[...], dl[d * 8 + ((x - o) % NX) * 2 + core_])
                unit = unit_of(piece)
                lanes = slice((2 * j + core_) * C, (2 * j + core_ + 1) * C)
                dft[p, :, lanes] = piece
                y_out[p, :, lanes] = coded(piece, unit)
                yu_out[p, :, lanes] = unit
        copies = []
        for o in (1, 2, 3):
            quarter = pl.ds(pl.multiple_of(((y + o) % NY) * QD, QD), QD)
            copies.append(remote(y_out.at[p, quarter, :], y_in.at[p, o - 1], y_peer(o)))
            copies.append(remote(yu_out.at[p], yu_in.at[p, o - 1], y_peer(o)))
        y_copies.append(copies)

    def head_part(half):
        total = None
        for pair in range(4):
            both = jnp.concatenate([dl[half * 8 + 2 * pair], dl[half * 8 + 2 * pair + 1]], axis=1)
            start = pl.multiple_of(half * T + pair * 2 * C, 2 * C)
            product = plain_dot(both, fin[pl.ds(start, 2 * C), :])
            total = product if total is None else total + product
        return total

    hg[d] = head_part(d)

    dl_cross.wait_recv()
    other_x = spread_x(od, col)

    z_copies = []
    for p in range(2):
        for copy in y_copies[p]:
            copy.wait_recv()
        quarter = dft[p, pl.ds(pl.multiple_of(y * QD, QD), QD), :]
        for o in (1, 2, 3):
            quarter = quarter + decoded(y_in[p, o - 1], yu_in[p, o - 1])
        dft[p, 0:QD, :] = quarter
        unit = unit_of(quarter)
        zu_out[p] = unit
        z_out[p] = coded(quarter, unit)
        copies = []
        for o in range(1, NZ):
            block = pl.ds(pl.multiple_of(((z + o) % NZ) * BD, BD), BD)
            copies.append(remote(z_out.at[p, block, :], z_in.at[p, o - 1], z_peer(o)))
            copies.append(remote(zu_out.at[p], zu_in.at[p, o - 1], z_peer(o)))
        z_copies.append(copies)

    hid_cross.wait_recv()
    hid_cols = [
        remote(hid.at[od, :, hq], hid.at[od, :, hq], (d, row, (col + o) % 8)) for o in range(1, 8)
    ]
    other_core = [other_x[3]] + [pass_core(od, other_x, o) for o in (1, 3, 2)]

    for p in range(2):
        for copy in z_copies[p]:
            copy.wait_recv()
        block = dft[p, pl.ds(pl.multiple_of(z * BD, BD), BD), :]
        for o in range(1, NZ):
            block = block + decoded(z_in[p, o - 1], zu_in[p, o - 1])
        dfb[y, zz, :, p * 512 : p * 512 + 512] = block.astype(BF16)

    def block_to(b, device):
        return remote(dfb.at[y, b], dfb.at[y, b], device)

    along_y = []

    def share_y(b):
        for o in (1, 2, 3):
            along_y.append(block_to(b, y_peer(o)))

    far = {o: block_to(zz, ring(o)) for o in (8, 4, -4)}
    near = {(o, 0): block_to(zz, ring(o)) for o in (1, -1, 2)}
    share_y(zz)
    for copy in fin_y + other_core:
        copy.wait_recv()
    hg[od] = head_part(od)
    for o in (1, -1, 2):
        near[o, 0].wait_recv()
        share_y((zz - o) % (2 * NZ))
    for q in (4, -4, 8):
        far[q].wait_recv()
        b = (zz - q) % (2 * NZ)
        for o in (1, -1, 2):
            near[o, q] = block_to(b, ring(o))
        share_y(b)
    hg[0] = hg[0] + hg[1]
    for q in (4, -4, 8):
        for o in (1, -1, 2):
            near[o, q].wait_recv()
            share_y((zz - o - q) % (2 * NZ))
    for copy in hid_cols:
        copy.wait_recv()
    for copy in along_y:
        copy.wait_recv()
    down = None
    for half in range(2):
        for p, offsets in enumerate(PARTS):
            for j, o in enumerate(offsets):
                tokens = pl.ds(pl.multiple_of(((x - o) % NX) * 2 * C, 2 * C), 2 * C)
                first = p * 512 + j * 256
                right = dfb[:, half * NZ : half * NZ + NZ, :, first : first + 256].reshape(D, 2 * C)
                product = tokens_dot(hid[half, :, tokens], right)
                down = product if down is None else down + product

    rtile[col] = jnp.zeros((8, 128), F32)
    hsq = hg[0] * hg[0]
    dsq = down * down
    mine = rtile.at[col]
    lanes_to_tile(mine, 0, column_to_lanes(jnp.sum(hsq, axis=1, keepdims=True)))
    down_lanes = column_to_lanes(jnp.sum(dsq, axis=1, keepdims=True))
    mine[4:5, :] = down_lanes[:, 0:128]
    mine[5:6, :] = down_lanes[:, 128:256]
    mine[6:7, 0:64] = down_lanes[:, 256:320]
    copies = [remote(rtile.at[col], rtile.at[col], (d, row, (col + o) % 8)) for o in range(1, 8)]
    for copy in copies:
        copy.wait_recv()
    rsum = jnp.sum(rtile[...], axis=0)
    hr = DECAY_RATE * hro[...].reshape(1, V) + (1.0 - DECAY_RATE) * (
        tile_to_lanes(rsum, 0, 4) * (1.0 / FULL_D) + EPS_SQUARE
    )
    dr = DECAY_RATE * dro[...].reshape(1, FF) + (1.0 - DECAY_RATE) * (
        tile_to_lanes(rsum, 4, 3)[:, 0:FF] * (1.0 / FULL_D) + EPS_SQUARE
    )
    hrows[...] = hr
    drows[...] = dr
    hr_col = lanes_to_column(hr)
    dr_col = lanes_to_column(dr)

    mine = ctile.at[y]
    lanes_to_tile(mine, 0, jnp.sum(hsq, axis=0, keepdims=True))
    lanes_to_tile(mine, 4, jnp.sum(dsq, axis=0, keepdims=True))
    lanes_to_tile(mine, 8, jnp.sum(hsq / hr_col, axis=0, keepdims=True))
    lanes_to_tile(mine, 12, jnp.sum(dsq / dr_col, axis=0, keepdims=True))
    copies = [remote(ctile.at[y], ctile.at[y], y_peer(o)) for o in (1, 2, 3)]
    for copy in copies:
        copy.wait_recv()
    ztile[z] = jnp.sum(ctile[...], axis=0)
    copies = [remote(ztile.at[z], ztile.at[z], z_peer(o)) for o in range(1, NZ)]
    for copy in copies:
        copy.wait_recv()
    csum = jnp.sum(ztile[...], axis=0)
    hc = DECAY_RATE * hco[...].reshape(1, D) + (1.0 - DECAY_RATE) * (
        tile_to_lanes(csum, 0, 4) * (1.0 / FULL_V) + EPS_SQUARE
    )
    dc = DECAY_RATE * dco[...].reshape(1, D) + (1.0 - DECAY_RATE) * (
        tile_to_lanes(csum, 4, 4) * (1.0 / FULL_FF) + EPS_SQUARE
    )
    hcols[...] = hc
    dcols[...] = dc
    hs = jnp.sum(tile_to_lanes(csum, 8, 4) / hc, axis=1, keepdims=True)
    ds = jnp.sum(tile_to_lanes(csum, 12, 4) / dc, axis=1, keepdims=True)
    stile[col, 0:1, :] = jnp.broadcast_to(hs, (1, 128))
    stile[col, 1:2, :] = jnp.broadcast_to(ds, (1, 128))
    copies = [remote(stile.at[col], stile.at[col], (d, row, (col + o) % 8)) for o in range(1, 8)]
    hup[...] = hg[0] * lax.rsqrt(hr_col) * lax.rsqrt(hc)
    dup[...] = down * lax.rsqrt(dr_col) * lax.rsqrt(dc)
    for copy in copies:
        copy.wait_recv()
    clips[...] = jnp.sum(stile[...], axis=0)

    for copy in pending:
        copy.wait_send()

    @pl.loop(1, 32)
    def _(o):
        stat_copy(o).wait_send()


def finish(hraw, hr, hc, draw, dr, dc, squares, hup, hrows, hcols, dup, drows, dcols):
    def clip(square_total, entries):
        return 1.0 / jnp.maximum(1.0, jnp.sqrt(square_total * (1.0 / entries)) / CLIP_LEVEL)

    hup[...] = hraw[...] * clip(squares[0:1, 0:1], FULL_V * FULL_D)
    dup[...] = draw[...] * clip(squares[1:2, 0:1], FULL_FF * FULL_D)
    hrows[...] = hr[...].reshape(V)
    hcols[...] = hc[...].reshape(D)
    drows[...] = dr[...].reshape(FF)
    dcols[...] = dc[...].reshape(D)


N_SEM = 256


def local(fin, w, hid, tgt, hro, hco, dro, dco):
    sds = jax.ShapeDtypeStruct
    vm = pltpu.VMEM
    hbm = pl.BlockSpec(memory_space=pl.ANY)
    vmem = pl.BlockSpec(memory_space=pltpu.VMEM)
    raw = pl.pallas_call(
        body,
        out_shape=(
            sds((V, D), F32), sds((1, V), F32), sds((1, D), F32),
            sds((FF, D), F32), sds((1, FF), F32), sds((1, D), F32), sds((2, 128), F32),
        ),
        in_specs=[hbm] * 3 + [vmem] * 5,
        out_specs=(vmem,) * 7,
        scratch_shapes=[
            vm((2 * T, D), BF16),
            vm((V, D), BF16),
            vm((D, V), BF16),
            vm((2, FF, T), BF16),
            vm((16, V, C), BF16),
            vm((4, V, C), F32),
            vm((4, V, C), F32),
            vm((4, V, C), F32),
            vm((3, V, C), I16),
            vm((3, V, C), I16),
            vm((3, 1, C), F32),
            vm((3, 1, C), F32),
            vm((32, 2, C), F32),
            vm((2, D, T // 2), F32),
            vm((2, D, T // 2), I16),
            vm((2, 3, QD, T // 2), I16),
            vm((2, 1, T // 2), F32),
            vm((2, 3, 1, T // 2), F32),
            vm((2, QD, T // 2), I16),
            vm((2, NZ - 1, BD, T // 2), I16),
            vm((2, 1, T // 2), F32),
            vm((2, NZ - 1, 1, T // 2), F32),
            vm((NY, 2 * NZ, BD, T), BF16),
            vm((2, V, D), F32),
            vm((8, 8, 128), F32),
            vm((NY, 16, 128), F32),
            vm((NZ, 16, 128), F32),
            vm((8, 2, 128), F32),
            pltpu.SemaphoreType.DMA((3,)),
            pltpu.SemaphoreType.DMA((N_SEM,)),
            pltpu.SemaphoreType.DMA((N_SEM,)),
        ],
        compiler_params=pltpu.CompilerParams(
            collective_id=0, has_side_effects=True, vmem_limit_bytes=56 << 20
        ),
    )(fin, w, hid.T, tgt.reshape(8, C), hro, hco, dro, dco)
    return pl.pallas_call(
        finish,
        out_shape=(
            sds((V, D), F32), sds((V,), F32), sds((D,), F32),
            sds((FF, D), F32), sds((FF,), F32), sds((D,), F32),
        ),
        in_specs=[vmem] * 7,
        out_specs=(vmem,) * 6,
        compiler_params=pltpu.CompilerParams(vmem_limit_bytes=16 << 20),
    )(*raw)


def solution(mesh):
    return jax.shard_map(
        local,
        mesh=mesh,
        in_specs=(
            P("dp", "col"),
            P("row", "col"),
            P("dp", "row"),
            P("dp"),
            P("row"),
            P("col"),
            P("row"),
            P("col"),
        ),
        out_specs=(P("row", "col"), P("row"), P("col"), P("row", "col"), P("row"), P("col")),
        check_vma=False,
    )
```

time: 162 us -> 152 us (0.938)
  local copies, waits for them, and re-layouts: 9.17 us -> 2.99 us
  Pallas kernels: 151 us -> 148 us
    unnamed x18 -> x14, local copies, waits for them, and re-layouts: 8.61 us -> 2.99 us
    pallas_call x1, Pallas kernels: 151 us -> 147 us  [local(): pl.pallas_call(body, out_shape=(sds((V, D), F32), sds((1, V), F32), sds((...]
where the time goes in v2:
time: 152 us
  Pallas kernels  148 us (97%)
  local copies, waits for them, and re-layouts  2.99 us (2%)
    pallas_call x1, Pallas kernels, local(): pl.pallas_call(body, out_shape=(sds((V, D), F32), sds((1, V), F32), sds((...  147 us

profile of v2, /device:TPU:1, one launch (start us, length us, event | category | flops | bytes accessed | tf_op | source)
XLA Modules:
  0.0 151.7 jit_solution(3281208112260295927)
XLA Ops:
  0.6 146.8 %shard_map.127 = (f32[512,512]{1,0:T(8,128)}, f32[1,512]{1,0:T(1,128)}, f32[1,512]{1,0:T(1,128)}, f32[320,512]{1,0:T(8,128)}, f32[1,320]{1,0:T(1,128)}, /*index=5*/f32[1,512]{1,0:T(1,128)}, f32[2,128]{1,0:T(2,128)}) custom-call(bf16[1024,512]{1,0:T(8,128)(2,1)} %fin_in.1, bf16[512,512]{1,0:T(8,128)(2,1)} %w_in.1, bf16[320,1024]{1,0:T(8,128)(2,1)} %bitcast.2, ...), custom_call_target="tpu_custom_call" | custom-call | tf_op jit(solution)/shard_map/pallas_call | solution.py:427
  147.4 0.0 copy-start.6
  147.4 0.0 copy-start.4
  147.4 0.0 copy-start.3
  147.4 0.0 copy-start.2
  147.4 0.0 copy-start.5
  147.5 0.6 copy-done.6
  148.1 0.0 copy-done.4
  148.1 0.0 copy-done.3
  148.1 0.0 copy-done.2
  148.1 0.0 copy-done.5
  148.1 0.0 copy-start
  148.1 1.2 copy-done
  149.3 0.0 copy-start.1
  149.3 1.1 copy-done.1
  150.4 1.3 shard_map.128
Async XLA Ops:
  147.4 0.7 copy-start.6
  147.4 0.7 copy-start.4
  147.4 0.7 copy-start.3
  147.4 0.7 copy-start.2
  147.4 0.7 copy-start.5
  148.1 1.2 copy-start
  149.3 1.1 copy-start.1

commit v3 on v2

--- a/solution.py
+++ b/solution.py
@@ -66,9 +66,9 @@
     fin_in, w_in, hid_in, tgt, hro, hco, dro, dco,
     hup, hrows, hcols, dup, drows, dcols, clips,
     fin, w, wt, hid, dl,
-    part, core_out, core_in, x_out, x_in, xu_out, xu_in,
+    both, core_in, x_out, x_in, xu_out, xu_in,
     stat, dft, y_out, y_in, yu_out, yu_in, z_out, z_in, zu_out, zu_in,
-    dfb, hg, rtile, ctile, ztile, stile,
+    dfb, hg, dq, d_out, d_in, du_out, du_in, rtile, ctile, ztile, stile,
     local_sem, send_sem, recv_sem,
 ):
     d, row, col = lax.axis_index("dp"), lax.axis_index("row"), lax.axis_index("col")
@@ -94,6 +94,7 @@
 
     core = (d, row, 2 * x + 1 - k)
     dp_peer = (od, row, col)
+    mirror = at(od, NZ - 1 - z, y, col)
 
     pending = []
     count = [0]
@@ -113,7 +114,7 @@
     loads = [
         pltpu.make_async_copy(fin_in, fin.at[pl.ds(d * T, T), :], local_sem.at[0]),
         pltpu.make_async_copy(w_in, w, local_sem.at[1]),
-        pltpu.make_async_copy(hid_in, hid.at[d], local_sem.at[2]),
+        pltpu.make_async_copy(hid_in, hid.at[d, y], local_sem.at[2]),
     ]
     for load in loads:
         load.start()
@@ -131,32 +132,31 @@
     def _(o):
         greet((d, row, (col + o) % 8))
 
-    @pl.loop(0, NZ)
-    def _(o):
-        greet(at(od, o, y, col))
+    others = [dp_peer, mirror] + [ring(o) for o in (1, -1, 2, -2, 4, -4)]
+    for device in others:
+        greet(device)
 
     for load in loads:
         load.wait()
 
-    def logits_part(c):
-        start = pl.multiple_of(d * T + c * C, C)
-        return tokens_dot(w[...], fin[pl.ds(start, C), :])
-
     for o in (1, 2, 3, 0):
-        xo = (x + o) % NX
-        core_out[o] = logits_part(2 * xo + 1 - k)
-        part[o] = logits_part(2 * xo + k)
+        start = pl.multiple_of(d * T + ((x + o) % NX) * 2 * C, 2 * C)
+        pair = tokens_dot(w[...], fin[pl.ds(start, 2 * C), :])
+        both[0, o] = pair[:, 0:C]
+        both[1, o] = pair[:, C : 2 * C]
+    part = both.at[k]
     wt[...] = w[...].T
-    pl.semaphore_wait(barrier, 31 + 7 + NZ)
+    pl.semaphore_wait(barrier, 31 + 7 + len(others))
 
     core_copies = {}
     for o in (1, 2, 3, 0):
-        core_copies[o] = remote(core_out.at[o], core_in.at[o], core)
-    fq = pl.multiple_of(d * T + (y * NZ + z) * 32, 32)
-    fin_cross = [
-        remote(fin.at[pl.ds(fq, 32), :], fin.at[pl.ds(fq, 32), :], at(od, (z + o) % NZ, y, col))
-        for o in range(NZ)
-    ]
+        core_copies[o] = remote(both.at[1 - k, o], core_in.at[o], core)
+    fq = pl.ds(pl.multiple_of(d * T + (y * NZ + z) * 32, 32), 32)
+    gq = pl.ds(pl.multiple_of(od * T + (y * NZ + NZ - 1 - z) * 32, 32), 32)
+    fin_cross = remote(fin.at[fq, :], fin.at[fq, :], mirror)
+    hq = pl.ds(pl.multiple_of(col * C, C), C)
+    hid_cross = remote(hid.at[d, y, :, hq], hid.at[d, y, :, hq], dp_peer)
+    hid_y = [remote(hid.at[d, y], hid.at[d, y], y_peer(o)) for o in (1, 2, 3)]
     x_copies = []
     for o in (1, 2, 3):
         core_copies[o].wait_recv()
@@ -168,6 +168,8 @@
         x_copies.append(remote(xu_out.at[o - 1], xu_in.at[o - 1], x_peer(o)))
     core_copies[0].wait_recv()
     part[0] = part[0] + core_in[0]
+    fin_cross.wait_recv()
+    fin_z = [remote(fin.at[gq, :], fin.at[gq, :], z_peer(o)) for o in range(1, NZ)]
 
     for copy in x_copies:
         copy.wait_recv()
@@ -220,17 +222,11 @@
 
     own_x = spread_x(d, col)
     dl_cross = remote(dl.at[me], dl.at[me], dp_peer)
-    hq = pl.ds(pl.multiple_of(col * C, C), C)
-    hid_cross = remote(hid.at[d, :, hq], hid.at[d, :, hq], dp_peer)
     own_core = {0: own_x[3]}
     own_core[1] = pass_core(d, own_x, 1)
-    for copy in fin_cross:
-        copy.wait_recv()
-    gy = pl.multiple_of(od * T + y * 256, 256)
-    fin_y = [
-        remote(fin.at[pl.ds(gy, 256), :], fin.at[pl.ds(gy, 256), :], y_peer(o)) for o in (1, 2, 3)
-    ]
     own_core[3] = pass_core(d, own_x, 3)
+    hid_cross.wait_recv()
+    hid_y += [remote(hid.at[od, y, :, hq], hid.at[od, y, :, hq], y_peer(o)) for o in (1, 2, 3)]
     own_core[2] = pass_core(d, own_x, 2)
 
     y_copies = []
@@ -251,6 +247,11 @@
             copies.append(remote(yu_out.at[p], yu_in.at[p, o - 1], y_peer(o)))
         y_copies.append(copies)
 
+    for copy in hid_y:
+        copy.wait_recv()
+    hid_x = [remote(hid.at[od, :, :, hq], hid.at[od, :, :, hq], x_peer(o)) for o in (1, 2, 3)]
+    hid_core = [remote(hid.at[od, :, :, hq], hid.at[od, :, :, hq], core)]
+
     def head_part(half):
         total = None
         for pair in range(4):
@@ -261,9 +262,6 @@
         return total
 
     hg[d] = head_part(d)
-
-    dl_cross.wait_recv()
-    other_x = spread_x(od, col)
 
     z_copies = []
     for p in range(2):
@@ -283,11 +281,12 @@
             copies.append(remote(zu_out.at[p], zu_in.at[p, o - 1], z_peer(o)))
         z_copies.append(copies)
 
-    hid_cross.wait_recv()
-    hid_cols = [
-        remote(hid.at[od, :, hq], hid.at[od, :, hq], (d, row, (col + o) % 8)) for o in range(1, 8)
-    ]
-    other_core = [other_x[3]] + [pass_core(od, other_x, o) for o in (1, 3, 2)]
+    for copy in fin_z:
+        copy.wait_recv()
+    gy = pl.ds(pl.multiple_of(od * T + y * 256, 256), 256)
+    fin_y = [remote(fin.at[gy, :], fin.at[gy, :], y_peer(o)) for o in (1, 2, 3)]
+    dl_cross.wait_recv()
+    other_x = spread_x(od, col)
 
     for p in range(2):
         for copy in z_copies[p]:
@@ -295,50 +294,62 @@
         block = dft[p, pl.ds(pl.multiple_of(z * BD, BD), BD), :]
         for o in range(1, NZ):
             block = block + decoded(z_in[p, o - 1], zu_in[p, o - 1])
-        dfb[y, zz, :, p * 512 : p * 512 + 512] = block.astype(BF16)
+        dfb[zz, :, p * 512 : p * 512 + 512] = block.astype(BF16)
 
     def block_to(b, device):
-        return remote(dfb.at[y, b], dfb.at[y, b], device)
-
-    along_y = []
-
-    def share_y(b):
-        for o in (1, 2, 3):
-            along_y.append(block_to(b, y_peer(o)))
-
-    far = {o: block_to(zz, ring(o)) for o in (8, 4, -4)}
-    near = {(o, 0): block_to(zz, ring(o)) for o in (1, -1, 2)}
-    share_y(zz)
-    for copy in fin_y + other_core:
-        copy.wait_recv()
-    hg[od] = head_part(od)
-    for o in (1, -1, 2):
-        near[o, 0].wait_recv()
-        share_y((zz - o) % (2 * NZ))
-    for q in (4, -4, 8):
-        far[q].wait_recv()
+        return remote(dfb.at[b], dfb.at[b], device)
+
+    near = {}
+
+    def pass_on(q):
         b = (zz - q) % (2 * NZ)
         for o in (1, -1, 2):
             near[o, q] = block_to(b, ring(o))
-        share_y(b)
+
+    far = {o: block_to(zz, ring(o)) for o in (8, 4, -4)}
+    pass_on(0)
+    other_core = [other_x[3]] + [pass_core(od, other_x, o) for o in (1, 3, 2)]
+    for q in (4, -4, 8):
+        far[q].wait_recv()
+        pass_on(q)
+    for o in (1, 3, 2):
+        hid_x[o - 1].wait_recv()
+        lanes = pl.ds(pl.multiple_of((((x - o) % NX) * 2 + k) * C, C), C)
+        hid_core.append(remote(hid.at[od, :, :, lanes], hid.at[od, :, :, lanes], core))
+    for copy in fin_y + other_core:
+        copy.wait_recv()
+    hg[od] = head_part(od)
     hg[0] = hg[0] + hg[1]
-    for q in (4, -4, 8):
-        for o in (1, -1, 2):
-            near[o, q].wait_recv()
-            share_y((zz - o - q) % (2 * NZ))
-    for copy in hid_cols:
-        copy.wait_recv()
-    for copy in along_y:
-        copy.wait_recv()
-    down = None
+    for copy in near.values():
+        copy.wait_recv()
+    for copy in hid_core:
+        copy.wait_recv()
+    total = None
     for half in range(2):
         for p, offsets in enumerate(PARTS):
             for j, o in enumerate(offsets):
                 tokens = pl.ds(pl.multiple_of(((x - o) % NX) * 2 * C, 2 * C), 2 * C)
                 first = p * 512 + j * 256
-                right = dfb[:, half * NZ : half * NZ + NZ, :, first : first + 256].reshape(D, 2 * C)
-                product = tokens_dot(hid[half, :, tokens], right)
-                down = product if down is None else down + product
+                right = dfb[half * NZ : half * NZ + NZ, :, first : first + 256].reshape(QD, 2 * C)
+                product = tokens_dot(hid[half, :, :, tokens].reshape(NY * FF, 2 * C), right)
+                total = product if total is None else total + product
+    dq[...] = total.reshape(NY, FF, QD)
+    unit = unit_of(total)
+    du_out[...] = unit
+    d_out[...] = coded(total, unit).reshape(NY, FF, QD)
+    swaps = []
+    for o in (1, 2, 3):
+        swaps.append(remote(d_out.at[(y + o) % NY], d_in.at[y], y_peer(o)))
+        swaps.append(remote(du_out, du_in.at[y], y_peer(o)))
+    mine = dq[y]
+    d_in[y] = d_out[y]
+    du_in[y] = unit
+    for copy in swaps:
+        copy.wait_recv()
+    for q in range(NY):
+        dq[q] = decoded(d_in[q], du_in[q])
+    dq[y] = mine
+    down = jnp.concatenate([dq[q] for q in range(NY)], axis=1)
 
     rtile[col] = jnp.zeros((8, 128), F32)
     hsq = hg[0] * hg[0]
@@ -436,10 +447,9 @@
             vm((2 * T, D), BF16),
             vm((V, D), BF16),
             vm((D, V), BF16),
-            vm((2, FF, T), BF16),
+            vm((2, NY, FF, T), BF16),
             vm((16, V, C), BF16),
-            vm((4, V, C), F32),
-            vm((4, V, C), F32),
+            vm((2, 4, V, C), F32),
             vm((4, V, C), F32),
             vm((3, V, C), I16),
             vm((3, V, C), I16),
@@ -455,8 +465,13 @@
             vm((2, NZ - 1, BD, T // 2), I16),
             vm((2, 1, T // 2), F32),
             vm((2, NZ - 1, 1, T // 2), F32),
-            vm((NY, 2 * NZ, BD, T), BF16),
+            vm((2 * NZ, BD, T), BF16),
             vm((2, V, D), F32),
+            vm((NY, FF, QD), F32),
+            vm((NY, FF, QD), I16),
+            vm((NY, FF, QD), I16),
+            vm((1, QD), F32),
+            vm((NY, 1, QD), F32),
             vm((8, 8, 128), F32),
             vm((NY, 16, 128), F32),
             vm((NZ, 16, 128), F32),

time: 152 us -> 134 us (0.88)
  Pallas kernels: 148 us -> 130 us
    pallas_call x1, Pallas kernels: 147 us -> 129 us  [local(): pl.pallas_call(body, out_shape=(sds((V, D), F32), sds((1, V), F32), sds((...]
where the time goes in v3:
time: 134 us
  Pallas kernels  130 us (97%)
  local copies, waits for them, and re-layouts  2.99 us (2%)
    pallas_call x1, Pallas kernels, local(): pl.pallas_call(body, out_shape=(sds((V, D), F32), sds((1, V), F32), sds((...  129 us
    unnamed x14, local copies, waits for them, and re-layouts  2.99 us

profile of v3, /device:TPU:1, one launch (start us, length us, event | category | flops | bytes accessed | tf_op | source)
XLA Modules:
  0.0 133.8 jit_solution(57691937312248606)
XLA Ops:
  0.6 128.8 %shard_map.127 = (f32[512,512]{1,0:T(8,128)}, f32[1,512]{1,0:T(1,128)}, f32[1,512]{1,0:T(1,128)}, f32[320,512]{1,0:T(8,128)}, f32[1,320]{1,0:T(1,128)}, /*index=5*/f32[1,512]{1,0:T(1,128)}, f32[2,128]{1,0:T(2,128)}) custom-call(bf16[1024,512]{1,0:T(8,128)(2,1)} %fin_in.1, bf16[512,512]{1,0:T(8,128)(2,1)} %w_in.1, bf16[320,1024]{1,0:T(8,128)(2,1)} %bitcast.2, ...), custom_call_target="tpu_custom_call" | custom-call | tf_op jit(solution)/shard_map/pallas_call | solution.py:438
  129.4 0.0 copy-start.6
  129.5 0.0 copy-start.4
  129.5 0.0 copy-start.3
  129.5 0.0 copy-start.2
  129.5 0.0 copy-start.5
  129.5 0.6 copy-done.6
  130.1 0.0 copy-done.4
  130.1 0.0 copy-done.3
  130.1 0.0 copy-done.2
  130.2 0.0 copy-done.5
  130.2 0.0 copy-start
  130.2 1.2 copy-done
  131.4 0.0 copy-start.1
  131.4 1.1 copy-done.1
  132.5 1.3 shard_map.128
Async XLA Ops:
  129.4 0.7 copy-start.6
  129.5 0.7 copy-start.4
  129.5 0.7 copy-start.3
  129.5 0.7 copy-start.2
  129.5 0.7 copy-start.5
  130.2 1.2 copy-start
  131.4 1.1 copy-start.1

commit v4 on v3

--- a/solution.py
+++ b/solution.py
@@ -68,7 +68,7 @@
     fin, w, wt, hid, dl,
     both, core_in, x_out, x_in, xu_out, xu_in,
     stat, dft, y_out, y_in, yu_out, yu_in, z_out, z_in, zu_out, zu_in,
-    dfb, hg, dq, d_out, d_in, du_out, du_in, rtile, ctile, ztile, stile,
+    dfb, hg, dq, d_out, d_in, du_out, du_in, htile, rtile, ctile, ztile, stile,
     local_sem, send_sem, recv_sem,
 ):
     d, row, col = lax.axis_index("dp"), lax.axis_index("row"), lax.axis_index("col")
@@ -320,6 +320,11 @@
         copy.wait_recv()
     hg[od] = head_part(od)
     hg[0] = hg[0] + hg[1]
+    hsq = hg[0] * hg[0]
+    lanes_to_tile(htile.at[col], 0, column_to_lanes(jnp.sum(hsq, axis=1, keepdims=True)))
+    head_copies = [
+        remote(htile.at[col], htile.at[col], (d, row, (col + o) % 8)) for o in range(1, 8)
+    ]
     for copy in near.values():
         copy.wait_recv()
     for copy in hid_core:
@@ -344,6 +349,16 @@
     mine = dq[y]
     d_in[y] = d_out[y]
     du_in[y] = unit
+    for copy in head_copies:
+        copy.wait_recv()
+    hr = DECAY_RATE * hro[...].reshape(1, V) + (1.0 - DECAY_RATE) * (
+        tile_to_lanes(jnp.sum(htile[...], axis=0), 0, 4) * (1.0 / FULL_D) + EPS_SQUARE
+    )
+    hrows[...] = hr
+    hr_col = lanes_to_column(hr)
+    lanes_to_tile(ctile.at[y], 0, jnp.sum(hsq, axis=0, keepdims=True))
+    lanes_to_tile(ctile.at[y], 8, jnp.sum(hsq / hr_col, axis=0, keepdims=True))
+    hup[...] = hg[0] * lax.rsqrt(hr_col)
     for copy in swaps:
         copy.wait_recv()
     for q in range(NY):
@@ -351,34 +366,25 @@
     dq[y] = mine
     down = jnp.concatenate([dq[q] for q in range(NY)], axis=1)
 
-    rtile[col] = jnp.zeros((8, 128), F32)
-    hsq = hg[0] * hg[0]
+    rtile[col] = jnp.zeros((4, 128), F32)
     dsq = down * down
     mine = rtile.at[col]
-    lanes_to_tile(mine, 0, column_to_lanes(jnp.sum(hsq, axis=1, keepdims=True)))
     down_lanes = column_to_lanes(jnp.sum(dsq, axis=1, keepdims=True))
-    mine[4:5, :] = down_lanes[:, 0:128]
-    mine[5:6, :] = down_lanes[:, 128:256]
-    mine[6:7, 0:64] = down_lanes[:, 256:320]
+    mine[0:1, :] = down_lanes[:, 0:128]
+    mine[1:2, :] = down_lanes[:, 128:256]
+    mine[2:3, 0:64] = down_lanes[:, 256:320]
     copies = [remote(rtile.at[col], rtile.at[col], (d, row, (col + o) % 8)) for o in range(1, 8)]
     for copy in copies:
         copy.wait_recv()
     rsum = jnp.sum(rtile[...], axis=0)
-    hr = DECAY_RATE * hro[...].reshape(1, V) + (1.0 - DECAY_RATE) * (
-        tile_to_lanes(rsum, 0, 4) * (1.0 / FULL_D) + EPS_SQUARE
+    dr = DECAY_RATE * dro[...].reshape(1, FF) + (1.0 - DECAY_RATE) * (
+        tile_to_lanes(rsum, 0, 3)[:, 0:FF] * (1.0 / FULL_D) + EPS_SQUARE
     )
-    dr = DECAY_RATE * dro[...].reshape(1, FF) + (1.0 - DECAY_RATE) * (
-        tile_to_lanes(rsum, 4, 3)[:, 0:FF] * (1.0 / FULL_D) + EPS_SQUARE
-    )
-    hrows[...] = hr
     drows[...] = dr
-    hr_col = lanes_to_column(hr)
     dr_col = lanes_to_column(dr)
 
     mine = ctile.at[y]
-    lanes_to_tile(mine, 0, jnp.sum(hsq, axis=0, keepdims=True))
     lanes_to_tile(mine, 4, jnp.sum(dsq, axis=0, keepdims=True))
-    lanes_to_tile(mine, 8, jnp.sum(hsq / hr_col, axis=0, keepdims=True))
     lanes_to_tile(mine, 12, jnp.sum(dsq / dr_col, axis=0, keepdims=True))
     copies = [remote(ctile.at[y], ctile.at[y], y_peer(o)) for o in (1, 2, 3)]
     for copy in copies:
@@ -401,7 +407,7 @@
     stile[col, 0:1, :] = jnp.broadcast_to(hs, (1, 128))
     stile[col, 1:2, :] = jnp.broadcast_to(ds, (1, 128))
     copies = [remote(stile.at[col], stile.at[col], (d, row, (col + o) % 8)) for o in range(1, 8)]
-    hup[...] = hg[0] * lax.rsqrt(hr_col) * lax.rsqrt(hc)
+    hup[...] = hup[...] * lax.rsqrt(hc)
     dup[...] = down * lax.rsqrt(dr_col) * lax.rsqrt(dc)
     for copy in copies:
         copy.wait_recv()
@@ -472,7 +478,8 @@
             vm((NY, FF, QD), I16),
             vm((1, QD), F32),
             vm((NY, 1, QD), F32),
-            vm((8, 8, 128), F32),
+            vm((8, 4, 128), F32),
+            vm((8, 4, 128), F32),
             vm((NY, 16, 128), F32),
             vm((NZ, 16, 128), F32),
             vm((8, 2, 128), F32),
@@ -492,7 +499,7 @@
         ),
         in_specs=[vmem] * 7,
         out_specs=(vmem,) * 6,
-        compiler_params=pltpu.CompilerParams(vmem_limit_bytes=16 << 20),
+        compiler_params=pltpu.CompilerParams(vmem_limit_bytes=60 << 20),
     )(*raw)
 
 

time: 134 us -> 132 us (0.985)
  local copies, waits for them, and re-layouts: 2.99 us -> 0 us
    unnamed x14 -> x0, local copies, waits for them, and re-layouts: 2.99 us -> none
    pallas_call x1, Pallas kernels: 1.3 us -> 2.75 us  [local(): pl.pallas_call(finish, out_shape=(sds((V, D), F32), sds((V,), F32), sds((...]
where the time goes in v4:
time: 132 us
  Pallas kernels  131 us (99%)
    pallas_call x1, Pallas kernels, local(): pl.pallas_call(body, out_shape=(sds((V, D), F32), sds((1, V), F32), sds((...  128 us
    pallas_call x1, Pallas kernels, local(): pl.pallas_call(finish, out_shape=(sds((V, D), F32), sds((V,), F32), sds((...  2.75 us

profile of v4, /device:TPU:1, one launch (start us, length us, event | category | flops | bytes accessed | tf_op | source)
XLA Modules:
  0.0 131.8 jit_solution(12391017422756968238)
XLA Ops:
  0.6 128.4 %shard_map.127 = (f32[512,512]{1,0:T(8,128)}, f32[1,512]{1,0:T(1,128)}, f32[1,512]{1,0:T(1,128)}, f32[320,512]{1,0:T(8,128)}, f32[1,320]{1,0:T(1,128)}, /*index=5*/f32[1,512]{1,0:T(1,128)}, f32[2,128]{1,0:T(2,128)}) custom-call(bf16[1024,512]{1,0:T(8,128)(2,1)} %fin_in.1, bf16[512,512]{1,0:T(8,128)(2,1)} %w_in.1, bf16[320,1024]{1,0:T(8,128)(2,1)} %bitcast.2, ...), custom_call_target="tpu_custom_call" | custom-call | tf_op jit(solution)/shard_map/pallas_call | solution.py:444
  129.1 2.7 %shard_map.128 = (f32[512,512]{1,0:T(8,128)}, f32[512]{0:T(512)}, f32[512]{0:T(512)}, f32[320,512]{1,0:T(8,128)}, f32[320]{0:T(512)}, /*index=5*/f32[512]{0:T(512)}) custom-call(f32[512,512]{1,0:T(8,128)} %get-tuple-element.13.hraw, f32[1,512]{1,0:T(1,128)} %get-tuple-element.14.hr, f32[1,512]{1,0:T(1,128)} %get-tuple-element.15.hc, ...), custom_call_target="tpu_custom_call" | custom-call | tf_op jit(solution)/shard_map/pallas_call | solution.py:494

commit v5 on v4

--- a/solution.py
+++ b/solution.py
@@ -124,20 +124,20 @@
     def greet(device):
         pl.semaphore_signal(barrier, inc=1, device_id=device, device_id_type=MESH)
 
-    @pl.loop(1, 32)
+    others = [dp_peer, mirror] + [ring(o) for o in (4, -4, 2, -2, 1, -1)]
+    for device in others:
+        greet(device)
+
+    @pl.loop(0, 31)
     def _(o):
-        greet((d, (row + o) % 32, col))
+        greet((d, (row + 1 + (o + 12) % 31) % 32, col))
 
     @pl.loop(1, 8)
     def _(o):
         greet((d, row, (col + o) % 8))
 
-    others = [dp_peer, mirror] + [ring(o) for o in (1, -1, 2, -2, 4, -4)]
-    for device in others:
-        greet(device)
-
-    for load in loads:
-        load.wait()
+    loads[0].wait()
+    loads[1].wait()
 
     for o in (1, 2, 3, 0):
         start = pl.multiple_of(d * T + ((x + o) % NX) * 2 * C, 2 * C)
@@ -145,7 +145,7 @@
         both[0, o] = pair[:, 0:C]
         both[1, o] = pair[:, C : 2 * C]
     part = both.at[k]
-    wt[...] = w[...].T
+    loads[2].wait()
     pl.semaphore_wait(barrier, 31 + 7 + len(others))
 
     core_copies = {}
@@ -157,6 +157,7 @@
     hq = pl.ds(pl.multiple_of(col * C, C), C)
     hid_cross = remote(hid.at[d, y, :, hq], hid.at[d, y, :, hq], dp_peer)
     hid_y = [remote(hid.at[d, y], hid.at[d, y], y_peer(o)) for o in (1, 2, 3)]
+    wt[...] = w[...].T
     x_copies = []
     for o in (1, 2, 3):
         core_copies[o].wait_recv()
@@ -261,8 +262,6 @@
             total = product if total is None else total + product
         return total
 
-    hg[d] = head_part(d)
-
     z_copies = []
     for p in range(2):
         for copy in y_copies[p]:
@@ -287,6 +286,7 @@
     fin_y = [remote(fin.at[gy, :], fin.at[gy, :], y_peer(o)) for o in (1, 2, 3)]
     dl_cross.wait_recv()
     other_x = spread_x(od, col)
+    hg[d] = head_part(d)
 
     for p in range(2):
         for copy in z_copies[p]:

time: 132 us -> 132 us (level)
  no operation moved by 1% of the time
where the time goes in v5:
time: 132 us; the launch traced here: 131 us
  Pallas kernels  131 us (99%)
    pallas_call x1, Pallas kernels, local(): pl.pallas_call(body, out_shape=(sds((V, D), F32), sds((1, V), F32), sds((...  128 us
    pallas_call x1, Pallas kernels, local(): pl.pallas_call(finish, out_shape=(sds((V, D), F32), sds((V,), F32), sds((...  2.75 us

profile of v5, /device:TPU:1, one launch (start us, length us, event | category | flops | bytes accessed | tf_op | source)
XLA Modules:
  0.0 131.4 jit_solution(3349679825395441209)
XLA Ops:
  0.6 128.0 %shard_map.127 = (f32[512,512]{1,0:T(8,128)}, f32[1,512]{1,0:T(1,128)}, f32[1,512]{1,0:T(1,128)}, f32[320,512]{1,0:T(8,128)}, f32[1,320]{1,0:T(1,128)}, /*index=5*/f32[1,512]{1,0:T(1,128)}, f32[2,128]{1,0:T(2,128)}) custom-call(bf16[1024,512]{1,0:T(8,128)(2,1)} %fin_in.1, bf16[512,512]{1,0:T(8,128)(2,1)} %w_in.1, bf16[320,1024]{1,0:T(8,128)(2,1)} %bitcast.2, ...), custom_call_target="tpu_custom_call" | custom-call | tf_op jit(solution)/shard_map/pallas_call | solution.py:444
  128.6 2.7 %shard_map.128 = (f32[512,512]{1,0:T(8,128)}, f32[512]{0:T(512)}, f32[512]{0:T(512)}, f32[320,512]{1,0:T(8,128)}, f32[320]{0:T(512)}, /*index=5*/f32[512]{0:T(512)}) custom-call(f32[512,512]{1,0:T(8,128)} %get-tuple-element.13.hraw, f32[1,512]{1,0:T(1,128)} %get-tuple-element.14.hr, f32[1,512]{1,0:T(1,128)} %get-tuple-element.15.hc, ...), custom_call_target="tpu_custom_call" | custom-call | tf_op jit(solution)/shard_map/pallas_call | solution.py:494
